TPU v7x, 32 devices: a whole 2x2x4 slice. The times are simulated.
32 devices in a mesh: segment: 2 (over y), fsdp: 4 (over x, core), seq: 4 (over z).
Axes of the slice: x: 2, y: 2, z: 4, core: 2. Of those that a mesh axis runs over, the one named last changes fastest.
Arguments:
- arriving: bfloat16 [2, 4, 768, 2048], P('segment', 'fsdp', 'seq'), may hold values from -6 to 6
- gain: float32 [2, 2048], P('segment'), may hold values from 0.1 to 1.9
- input_weight: bfloat16 [2, 2048, 16, 3, 128], P('segment', 'fsdp', 'seq')
- output_weight: bfloat16 [2, 16, 128, 2048], P('segment', 'seq', None, 'fsdp'), may hold values from -1 to 1
- block_pattern: int32 [2, 4, 24, 6], P('segment', 'fsdp'), may hold values from 0 to 23, as said below
Outputs:
- passed: bfloat16 [2, 4, 768, 2048], P('segment', 'fsdp', 'seq')
Inputs may be any that keep to these rules, and one draw needn't show every extreme that they name: `block_pattern`: row j of a document lists 6 different blocks; the first three are j - 1, j and j + 1 modulo 24, and block 0 is listed in every row.
All inputs are finite; a program needn't handle non-finite values.
Results may differ from a plain program's by a relative error of at most 0.012.
Values may be sent and summed in bfloat16 or wider, within the bound.
A program may use at most 64 MiB of HBM per device.

v0:
```python
import jax
import jax.numpy as jnp
from jax import lax
from jax.sharding import PartitionSpec as P

BLOCK = 32
SEL = 6


EPSILON = 1e-05


def passed_along(value, axis, steps):
    count = lax.axis_size(axis)
    pairs = [(source, (source + steps) % count) for source in range(count)]
    return lax.ppermute(value, axis, pairs)


def normalize(tokens, gain_row):
    values = tokens.astype(jnp.float32)
    spread = jnp.mean(values * values, axis=-1, keepdims=True)
    return (values * lax.rsqrt(spread + EPSILON) * gain_row).astype(jnp.bfloat16)


def attend(projected, pattern_rows):
    length, head_group, triple, head_width = projected.shape
    block_count = length // BLOCK
    query_rows = projected[:, :, 0].reshape(block_count, BLOCK, head_group, head_width)
    key_blocks = projected[:, :, 1].reshape(block_count, BLOCK, head_group, head_width)
    value_blocks = projected[:, :, 2].reshape(block_count, BLOCK, head_group, head_width)
    key_rows = jnp.take(key_blocks, pattern_rows, axis=0).reshape(
        block_count, SEL * BLOCK, head_group, head_width
    )
    value_rows = jnp.take(value_blocks, pattern_rows, axis=0).reshape(
        block_count, SEL * BLOCK, head_group, head_width
    )
    scores = jnp.einsum(
        "qbge,qnge->gqbn", query_rows, key_rows, preferred_element_type=jnp.float32
    ) * head_width ** (-0.5)
    row_max = jnp.max(scores, axis=-1, keepdims=True)
    exponent = jnp.exp(scores - row_max)
    weights = (exponent / jnp.sum(exponent, axis=-1, keepdims=True)).astype(jnp.bfloat16)
    mixed_rows = jnp.einsum(
        "gqbn,qnge->qbge", weights, value_rows, preferred_element_type=jnp.float32
    )
    return mixed_rows.astype(jnp.bfloat16).reshape(length, head_group * head_width)


def body(arriving, gain, input_weight, output_weight, block_pattern):
    tokens = arriving[0, 0]
    row_count = tokens.shape[0]
    normed = normalize(tokens, gain[0])
    slab_rows, head_group, triple, head_size = input_weight.shape[1:]
    columns = head_group * triple * head_size
    panel_flat = input_weight[0].reshape(slab_rows, columns)
    length = row_count * lax.axis_size("seq")
    whole_panel = lax.all_gather(panel_flat, "fsdp", axis=0, tiled=True)
    projected = jnp.dot(
        lax.all_gather(normed, "seq", axis=0, tiled=True),
        whole_panel,
        preferred_element_type=jnp.float32,
    )
    projected = projected.astype(jnp.bfloat16).reshape(length, head_group, triple, head_size)
    mixed_rows = attend(projected, block_pattern[0, 0])
    out_panel = output_weight[0].reshape(head_group * head_size, -1)
    whole_out = lax.all_gather(out_panel, "fsdp", axis=1, tiled=True)
    branch = lax.psum_scatter(
        jnp.dot(mixed_rows, whole_out, preferred_element_type=jnp.float32).astype(jnp.bfloat16),
        "seq",
        scatter_dimension=0,
        tiled=True,
    ).astype(jnp.float32)
    updated = (tokens.astype(jnp.float32) + branch).astype(jnp.bfloat16)
    passed = passed_along(updated, "segment", 1)
    return passed[None, None]


def solution(mesh):
    in_specs = (
        P("segment", "fsdp", "seq", None),
        P("segment", None),
        P("segment", "fsdp", "seq", None, None),
        P("segment", "seq", None, "fsdp"),
        P("segment", "fsdp", None, None),
    )
    out_specs = P("segment", "fsdp", "seq", None)
    return jax.shard_map(body, mesh=mesh, in_specs=in_specs, out_specs=out_specs, check_vma=False)
```

profile of v0, /device:TPU:18, one launch (start us, length us, event | category | flops | bytes accessed | tf_op | source)
XLA Modules:
  0.0 275.5 jit_solution(2608817675597869169)
XLA Ops:
  6.5 1.5 fusion.4
  8.0 2.3 fusion.6
  10.3 0.0 all-gather.6.cloned.1.call-start
  10.4 2.6 copy.24
  13.0 0.0 all-gather.8.cloned.1.call-start
  13.0 0.7 all-gather.8.cloned.1.call-update
  13.7 0.0 reduce-scatter.2.cloned.1.call-start
  13.8 0.1 copy.27
  13.9 0.1 reshape.54
  14.0 0.1 copy.23
  14.1 59.6 %all-gather.4.cloned.1.call-done = bf16[768,2048]{1,0:T(8,128)(2,1)} async-done(((bf16[192,2048]{1,0:T(8,128)(2,1)}), bf16[768,2048]{1,0:T(8,128)(2,1)}) %all-gather.4.cloned.1.call-update) | async-done | bytes 3145744 | tf_op jit(solution)/shard_map/all_gather | solution.py:59
  73.7 47.0 %all-gather.6.cloned.1.call-done = bf16[2048,1536]{0,1:T(8,128)(2,1)} async-done(((bf16[512,1536]{0,1:T(8,128)(2,1)}), bf16[2048,1536]{0,1:T(8,128)(2,1)}) %all-gather.6.cloned.1.call-update) | async-done | bytes 6291472 | tf_op jit(solution)/shard_map/all_gather | solution.py:57
  120.7 9.3 %convolution_convert_fusion.1 = bf16[768,1536]{1,0:T(8,128)(2,1)} fusion(bf16[768,2048]{1,0:T(8,128)(2,1)} %all-gather.4.cloned.1.call-done, bf16[2048,1536]{0,1:T(8,128)(2,1)} %all-gather.6.cloned.1.call-done), kind=kOutput, calls=%fused_computation.6 | convolution fusion | flops 4833017856 | bytes 11796480 | tf_op jit(solution)/shard_map/dot_general | solution.py:58
  130.0 2.9 %copy.25 = bf16[768,1536]{0,1:T(8,128)(2,1)S(1)} copy(bf16[768,1536]{1,0:T(8,128)(2,1)} %convolution_convert_fusion.1) | data formatting | bytes 4718592 | tf_op jit(solution)/shard_map/convert_element_type | solution.py:63
  132.9 1.3 fusion.20
  134.2 1.5 copy.31
  135.8 1.5 copy.26
  137.3 7.6 %gather_fusion.1 = bf16[144,32,4,128]{3,1,2,0:T(8,128)(2,1)} fusion(bf16[24,32,4,128]{3,1,0,2:T(8,128)(2,1)S(1)} %bitcast.37, s32[1024]{0:T(1024)S(1)} %pad_clamp_fusion), kind=kCustom, calls=%fused_computation.1.clone | custom fusion | bytes 9437760 | tf_op jit(solution)/shard_map/jit(_take)/gather | solution.py:31
  144.8 7.6 %gather_fusion = bf16[144,32,4,128]{3,1,2,0:T(8,128)(2,1)} fusion(bf16[24,32,4,128]{3,1,0,2:T(8,128)(2,1)S(1)} %bitcast.36, s32[1024]{0:T(1024)S(1)} %pad_clamp_fusion), kind=kCustom, calls=%fused_computation.clone | custom fusion | bytes 9437760 | tf_op jit(solution)/shard_map/jit(_take)/gather | solution.py:34
  152.5 5.7 %broadcast_select_fusion = (bf16[24,6,32,4,128]{4,2,3,1,0:T(8,128)(2,1)S(1)}, bf16[24,6,32,4,128]{4,2,3,1,0:T(8,128)(2,1)}) fusion(bf16[24,6,32,4,128]{4,2,3,1,0:T(8,128)(2,1)} %bitcast.38, pred[24,6]{1,0:T(8,128)(4,1)S(1)} %copy.23, bf16[24,6,32,4,128]{4,2,3,1,0:T(8,128)(2,1)} %bitcast.39), kind=kLoop, calls=%fused_computation.3 | loop fusion | flops 4718592 | bytes 18874512 | tf_op jit(solution)/shard_map/jit(_take)/select_n | solution.py:31
  158.1 3.6 %copy.33 = bf16[24,6,32,4,128]{4,2,1,0,3:T(8,128)(2,1)} copy(bf16[24,6,32,4,128]{4,2,3,1,0:T(8,128)(2,1)S(1)} %get-tuple-element.9) | data formatting | bytes 9437184 | tf_op jit(solution)/shard_map/jit(_take)/select_n | solution.py:31
  161.7 0.4 copy.29
  162.0 5.9 %copy.28 = bf16[24,6,32,4,128]{4,2,1,3,0:T(8,128)(2,1)} copy(bf16[24,6,32,4,128]{4,2,3,1,0:T(8,128)(2,1)} %get-tuple-element.10) | data formatting | bytes 9437184 | tf_op jit(solution)/shard_map/jit(_take)/select_n | solution.py:34
  167.9 7.2 %fusion.21 = (f32[4,24,32]{2,1,0:T(8,128)S(1)}, f32[4,24,32,192]{3,2,1,0:T(8,128)}) fusion(bf16[24,32,4,128]{3,1,0,2:T(8,128)(2,1)S(1)} %bitcast.44, bf16[24,192,4,128]{3,1,0,2:T(8,128)(2,1)} %bitcast.40), kind=kOutput, calls=%fused_computation.31 | convolution fusion | flops 152764608 | bytes 7876608 | tf_op jit(solution)/shard_map/sub | solution.py:41
  175.1 5.2 %fusion.14 = bf16[24,32,4,128]{3,1,2,0:T(8,128)(2,1)S(1)} fusion(bf16[24,192,4,128]{3,1,2,0:T(8,128)(2,1)} %bitcast.43, f32[4,24,32,192]{3,2,1,0:T(8,128)} %get-tuple-element.12, f32[4,24,32]{2,1,0:T(8,128)S(1)} %get-tuple-element.11), kind=kOutput, calls=%fused_computation.22 | convolution fusion | flops 152567808 | bytes 7876608 | tf_op jit(solution)/shard_map/gqbn,qnge->qbge/dot_general | solution.py:43
  180.3 0.4 copy.35
  180.8 5.0 %convolution_convert_fusion = bf16[768,2048]{1,0:T(8,128)(2,1)} fusion(bf16[512,2048]{1,0:T(8,128)(2,1)} %all-gather.8.cloned.1.call-done, bf16[96,8,4,128]{3,2,1,0:T(4,128)(2,1)S(1)} %bitcast.45), kind=kOutput, calls=%fused_computation.5 | convolution fusion | flops 1612185600 | bytes 6029312 | tf_op jit(solution)/shard_map/dot_general | solution.py:68
  185.8 61.5 %reduce-scatter.2.cloned.1.call-done = bf16[192,2048]{1,0:T(8,128)(2,1)} async-done(((bf16[768,2048]{1,0:T(8,128)(2,1)}), bf16[192,2048]{1,0:T(8,128)(2,1)}) %reduce-scatter.2.cloned.1.call-update) | async-done | bytes 786448 | tf_op jit(solution)/shard_map/reduce_scatter | solution.py:67
  247.3 1.4 fusion.7
  248.7 1.6 collective-permute-start
  250.2 17.9 %collective-permute-done = bf16[192,2048]{1,0:T(8,128)(2,1)S(1)} collective-permute-done((bf16[192,2048]{1,0:T(8,128)(2,1)S(1)}, bf16[192,2048]{1,0:T(8,128)(2,1)S(1)}, u32[]{:S(2)}, u32[]{:S(2)}) %collective-permute-start) | collective-permute-done | bytes 786464 | tf_op jit(solution)/shard_map/ppermute | solution.py:16
  268.1 0.9 copy.52
  (15 shorter events, 0.1 us)
Async XLA Ops:
  6.5 3.8 %copy-start.1 = (bf16[1,512,4,3,128]{4,2,3,1,0:T(4,128)(2,1)S(1)}, bf16[1,512,4,3,128]{4,2,3,1,0:T(4,128)(2,1)}, u32[]{:S(2)}) copy-start(bf16[1,512,4,3,128]{4,2,3,1,0:T(4,128)(2,1)} %param.9) | copy-start | bytes 4718596
  6.5 67.2 %all-gather.4.cloned.1.call-start = ((), (), s32[]{:S(2)}) async-start(), calls=%async_computation.1 | async-start | bytes 3932160 | tf_op jit(solution)/shard_map/all_gather | solution.py:59
  10.3 3.5 %copy-start.2 = (s32[1,1,24,6]{2,1,3,0:T(1,128)S(1)}, s32[1,1,24,6]{2,1,3,0:T(1,128)}, u32[]{:S(2)}) copy-start(s32[1,1,24,6]{2,1,3,0:T(1,128)} %param.11) | copy-start | bytes 1732
  10.3 110.4 %all-gather.6.cloned.1.call-start = ((), (), s32[]{:S(2)}) async-start(), calls=%async_computation.2 | async-start | bytes 7864320 | tf_op jit(solution)/shard_map/all_gather | solution.py:57
  13.0 167.8 %all-gather.8.cloned.1.call-start = ((), (), s32[]{:S(2)}) async-start(), calls=%async_computation.3 | async-start | bytes 2621440 | tf_op jit(solution)/shard_map/all_gather | solution.py:66
  13.7 233.6 %reduce-scatter.2.cloned.1.call-start = ((), (), s32[]{:S(2)}) async-start(), calls=%async_computation.4 | async-start | bytes 3932160 | tf_op jit(solution)/shard_map/reduce_scatter | solution.py:67
  185.8 61.5 %copy-start = (bf16[1,1,192,2048]{3,2,1,0:T(8,128)(2,1)S(1)}, bf16[1,1,192,2048]{3,2,1,0:T(8,128)(2,1)}, u32[]{:S(2)}) copy-start(bf16[1,1,192,2048]{3,2,1,0:T(8,128)(2,1)} %param.7) | copy-start | bytes 2359300
  248.7 19.4 %collective-permute-start = (bf16[192,2048]{1,0:T(8,128)(2,1)S(1)}, bf16[192,2048]{1,0:T(8,128)(2,1)S(1)}, u32[]{:S(2)}, u32[]{:S(2)}) collective-permute-start(bf16[192,2048]{1,0:T(8,128)(2,1)S(1)} %fusion.7), channel_id=1, source_target_pairs={{0,16},{16,0},{1,17},{17,1},{2,18},{18,2},{3,19},{19,3},{4,20},{20... | collective-permute-start | bytes 2359304 | tf_op jit(solution)/shard_map/ppermute | solution.py:16
Sparse Core Ops, SparseCore 0:
  10.5 63.1 all-gather.3
  75.3 45.4 all-gather.5
  122.3 22.5 all-gather.7
  185.9 61.3 reduce-scatter.1
where the time goes:
time: 277 us; the launch traced here: 276 us
  waiting for transfers between devices  187 us (68%)
  local copies, waits for them, and re-layouts  36.4 us (13%)
  matrix products  26.6 us (10%)
  between operations  13.2 us (5%)
  other arithmetic  10.8 us (4%)
    reduce_scatter x1, waiting for transfers between devices, body(): lax.psum_scatter(jnp.dot(mixed_rows, whole_out, preferred_element_type=jn...  61.5 us
    all_gather x1, waiting for transfers between devices, body(): lax.all_gather(normed, 'seq', axis=0, tiled=True)  59.6 us
    all_gather x1, waiting for transfers between devices, body(): whole_panel = lax.all_gather(panel_flat, 'fsdp', axis=0, tiled=True)  47 us
    ppermute x1, waiting for transfers between devices, passed_along(): return lax.ppermute(value, axis, pairs)  17.9 us
    dot_general x1, matrix products, body(): jnp.dot(lax.all_gather(normed, 'seq', axis=0, tiled=True), whole_panel, p...  9.25 us
    gather x1, local copies, waits for them, and re-layouts, attend(): jnp.take(value_blocks, pattern_rows, axis=0)  7.62 us
    gather x1, local copies, waits for them, and re-layouts, attend(): jnp.take(key_blocks, pattern_rows, axis=0)  7.56 us
    sub x1, matrix products, attend(): exponent = jnp.exp(scores - row_max)  7.16 us
  transfers between devices with their start and end apart: 5, of which 4 were waited for; matrix products, arithmetic and copies ran while one was open for 23% of the time, Pallas kernels for 0%

commit v1 on v0

v1 whole, which is shorter than its diff:
```python
import functools

import jax
import jax.numpy as jnp
from jax import lax
from jax.experimental import pallas as pl
from jax.experimental.pallas import tpu as pltpu
from jax.sharding import PartitionSpec as P

BLOCK = 32
SEL = 6
PIECE = 32
EPSILON = 1e-05
MESH = pl.DeviceIdType.MESH


def kernel(
    S, F, Z, HG,
    x_ref, gain_ref, w_ref, o_ref, pat_ref, out_ref,
    tok, win, wout, qkv, bias, in_l, in_r, outb, mixed, fin, acc,
    local_sem, zs, zr, ws, wr, vs, vr, rs, rr, ys, yr,
):
    rows, depth = x_ref.shape
    length = rows * Z
    slab, columns = w_ref.shape
    head = columns // (3 * HG)
    width = o_ref.shape[1]
    pieces = rows // PIECE
    half = slab // 2
    X = F // 2
    f32 = jnp.float32

    s = lax.axis_index("segment")
    f = lax.axis_index("fsdp")
    p = lax.axis_index("seq")
    core = lax.rem(f, 2)
    chip = lax.div(f, 2)
    sibling = f + 1 - 2 * core
    up = lax.rem(s + 1, S)
    down = lax.rem(s + S - 1, S)

    own_w = pltpu.make_async_copy(
        w_ref, win.at[pl.ds(pl.multiple_of(f * slab, slab), slab), :], local_sem.at[0])
    own_o = pltpu.make_async_copy(o_ref, wout.at[f], local_sem.at[1])
    own_w.start()
    own_o.start()

    barrier = pltpu.get_barrier_semaphore()

    def greet(device):
        pl.semaphore_signal(barrier, inc=1, device_id=device, device_id_type=MESH)

    pl.when(p > 0)(lambda: greet({"seq": p - 1}))
    pl.when(p < Z - 1)(lambda: greet({"seq": p + 1}))
    greet({"fsdp": sibling})
    for d in range(1, X):
        greet({"fsdp": lax.rem(chip + d, X) * 2 + core})
    greet({"segment": up})
    if S > 2:
        greet({"segment": down})
    always = 1 + (X - 1) + (2 if S > 2 else 1)
    pl.semaphore_wait(barrier, always + jnp.where(p > 0, 1, 0) + jnp.where(p < Z - 1, 1, 0))

    def w_rows(g, k):
        return win.at[pl.ds(pl.multiple_of(g * slab + k * half, half), half), :]

    def w_copy(g, k, device, slot, own):
        src = w_ref.at[pl.ds(k * half, half), :] if own else w_rows(g, k)
        return pltpu.make_async_remote_copy(
            src_ref=src, dst_ref=w_rows(g, k), send_sem=ws.at[slot, k], recv_sem=wr.at[g, k],
            device_id={"fsdp": device}, device_id_type=MESH)

    def o_copy(g, device, slot, own):
        src = o_ref if own else wout.at[g]
        return pltpu.make_async_remote_copy(
            src_ref=src, dst_ref=wout.at[g], send_sem=vs.at[slot], recv_sem=vr.at[g],
            device_id={"fsdp": device}, device_id_type=MESH)

    def peer(d):
        return lax.rem(chip + d, X) * 2 + core

    def source(d):
        return lax.rem(chip + X - d, X) * 2 + core

    for k in range(2):
        for d in range(1, X):
            w_copy(f, k, peer(d), d - 1, True).start()
        w_copy(f, k, sibling, X - 1, True).start()

    def t_rows(c, j):
        return tok.at[pl.ds(pl.multiple_of(c * rows + j * PIECE, PIECE), PIECE), :]

    def t_copy(c, j, direction, step):
        device = p + 1 if direction == 0 else p - 1
        return pltpu.make_async_remote_copy(
            src_ref=t_rows(c, j), dst_ref=t_rows(c, j),
            send_sem=zs.at[direction, step, j], recv_sem=zr.at[direction, step, j],
            device_id={"seq": device}, device_id_type=MESH)

    def norm_piece(j, carry):
        values = x_ref[pl.ds(pl.multiple_of(j * PIECE, PIECE), PIECE), :].astype(f32)
        spread = jnp.mean(values * values, axis=-1, keepdims=True)
        t_rows(p, j)[...] = (values * lax.rsqrt(spread + EPSILON) * gain_ref[...]).astype(jnp.bfloat16)
        pl.when(p < Z - 1)(lambda: t_copy(p, j, 0, 0).start())
        pl.when(p > 0)(lambda: t_copy(p, j, 1, 0).start())
        return carry

    lax.fori_loop(0, pieces, norm_piece, 0)

    key_block = lax.broadcasted_iota(jnp.int32, (BLOCK, length), 1) // BLOCK

    def bias_rows(b, carry):
        hit = key_block == pat_ref[b, 0]
        for i in range(1, SEL):
            hit = jnp.logical_or(hit, key_block == pat_ref[b, i])
        bias[pl.ds(pl.multiple_of(b * BLOCK, BLOCK), BLOCK), :] = jnp.where(hit, 0.0, -1e30)
        return carry

    lax.fori_loop(0, length // BLOCK, bias_rows, 0)

    def receive(t, forward):
        def one(j, carry):
            @pl.when(t < p)
            def _():
                t_copy(p - 1 - t, j, 0, t).wait_recv()
                if forward:
                    pl.when(p < Z - 1)(lambda: t_copy(p - 1 - t, j, 0, t + 1).start())

            @pl.when(t < Z - 1 - p)
            def _():
                t_copy(p + 1 + t, j, 1, t).wait_recv()
                if forward:
                    pl.when(p > 0)(lambda: t_copy(p + 1 + t, j, 1, t + 1).start())
            return carry

        lax.fori_loop(0, pieces, one, 0)

    def forward_w(k):
        for d in range(1, X):
            w_copy(source(d), k, sibling, X - 1 + d, False).wait_recv()
            w_copy(source(d), k, sibling, X - 1 + d, False).start()

    for t in range(Z - 2):
        receive(t, True)
        if t < 2:
            forward_w(t)
    for k in range(min(2, Z - 2), 2):
        forward_w(k)
    for d in range(1, X):
        o_copy(f, peer(d), d - 1, True).start()
    o_copy(f, sibling, X - 1, True).start()
    own_w.wait()
    for k in range(2):
        for d in range(X):
            other = lax.rem(chip + d, X) * 2 + 1 - core
            w_copy(other, k, sibling, 0, False).wait_recv()

    def project(e, carry):
        d = lax.div(e, 2)
        side = lax.rem(e, 2)

        @pl.when(e == 2 * Z - 2)
        def _():
            receive(Z - 2, False)
        c = jnp.where(side == 0, p - d, p + d)
        valid = jnp.where(side == 0, d <= p, jnp.logical_and(d >= 1, d <= Z - 1 - p))

        @pl.when(valid)
        def _():
            at = pl.ds(pl.multiple_of(c * rows, rows), rows)

            def one(h, inner):
                cols = pl.ds(pl.multiple_of(h * 3 * head, 3 * head), 3 * head)
                qkv[at, cols] = jnp.dot(
                    tok[at, :], win[:, cols], preferred_element_type=f32).astype(jnp.bfloat16)
                return inner

            lax.fori_loop(0, HG, one, 0)
        return carry

    lax.fori_loop(0, 2 * Z, project, 0)

    for d in range(1, X):
        o_copy(source(d), sibling, X - 1 + d, False).wait_recv()
        o_copy(source(d), sibling, X - 1 + d, False).start()
    own_o.wait()
    for d in range(X):
        o_copy(lax.rem(chip + d, X) * 2 + 1 - core, sibling, 0, False).wait_recv()

    def partial(c):
        at = pl.ds(pl.multiple_of(c * rows, rows), rows)
        for h in range(HG):
            base = h * 3 * head
            q = qkv[at, base:base + head]
            k = qkv[:, base + head:base + 2 * head]
            v = qkv[:, base + 2 * head:base + 3 * head]
            scores = lax.dot_general(q, k, (((1,), (1,)), ((), ())), preferred_element_type=f32)
            scores = scores * head ** (-0.5) + bias[at, :]
            exponent = jnp.exp(scores - jnp.max(scores, axis=-1, keepdims=True))
            total = jnp.sum(exponent, axis=-1, keepdims=True)
            value = jnp.dot(exponent.astype(jnp.bfloat16), v, preferred_element_type=f32)
            mixed[:, h * head:(h + 1) * head] = (value / total).astype(jnp.bfloat16)
        for g in range(F):
            outb[c, :, g * width:(g + 1) * width] = jnp.dot(
                mixed[...], wout[g], preferred_element_type=f32).astype(jnp.bfloat16)

    def s_copy(c, j, direction):
        device = p + 1 if direction == 0 else p - 1
        inbox = in_l if direction == 0 else in_r
        at = pl.ds(pl.multiple_of(j * PIECE, PIECE), PIECE)
        return pltpu.make_async_remote_copy(
            src_ref=outb.at[c, at, :], dst_ref=inbox.at[c, at, :],
            send_sem=rs.at[direction, c, j], recv_sem=rr.at[direction, c, j],
            device_id={"seq": device}, device_id_type=MESH)

    def y_copy(j):
        at = pl.ds(pl.multiple_of(j * PIECE, PIECE), PIECE)
        return pltpu.make_async_remote_copy(
            src_ref=fin.at[at, :], dst_ref=out_ref.at[at, :], send_sem=ys.at[j], recv_sem=yr.at[j],
            device_id={"segment": up}, device_id_type=MESH)

    def add_in(c, j, inbox):
        at = pl.ds(pl.multiple_of(j * PIECE, PIECE), PIECE)
        outb[c, at, :] = (outb[c, at, :].astype(f32) + inbox[c, at, :].astype(f32)).astype(jnp.bfloat16)

    def reduce_step(u, carry):
        own = u == Z - 1
        right = Z - 1 - u
        goes_right = jnp.logical_and(jnp.logical_not(own), right > p)
        goes_left = jnp.logical_and(jnp.logical_not(own), u < p)

        def side_of(side, inner):
            c = jnp.where(side == 0, jnp.where(own, p, right), u)
            valid = jnp.where(side == 0, jnp.logical_or(own, goes_right), goes_left)
            pl.when(valid)(lambda: partial(c))
            return inner

        lax.fori_loop(0, 2, side_of, 0)

        def one(j, inner):
            @pl.when(goes_right)
            def _():
                @pl.when(p > 0)
                def _():
                    s_copy(right, j, 0).wait_recv()
                    add_in(right, j, in_l)
                s_copy(right, j, 0).start()

            @pl.when(goes_left)
            def _():
                @pl.when(p < Z - 1)
                def _():
                    s_copy(u, j, 1).wait_recv()
                    add_in(u, j, in_r)
                s_copy(u, j, 1).start()
            return inner

        lax.fori_loop(0, pieces, one, 0)
        return carry

    lax.fori_loop(0, Z, reduce_step, 0)

    def finish(j, carry):
        at = pl.ds(pl.multiple_of(j * PIECE, PIECE), PIECE)
        acc[...] = outb[p, at, :].astype(f32)

        @pl.when(p < Z - 1)
        def _():
            s_copy(p, j, 1).wait_recv()
            acc[...] += in_r[p, at, :].astype(f32)

        @pl.when(p > 0)
        def _():
            s_copy(p, j, 0).wait_recv()
            acc[...] += in_l[p, at, :].astype(f32)
        fin[at, :] = (x_ref[at, :].astype(f32) + acc[...]).astype(jnp.bfloat16)
        y_copy(j).start()
        return carry

    lax.fori_loop(0, pieces, finish, 0)

    for k in range(2):
        for slot in range(2 * X - 1):
            w_copy(f, k, sibling, slot, False).wait_send()
    for slot in range(2 * X - 1):
        o_copy(f, sibling, slot, False).wait_send()

    def sent(j, carry):
        for t in range(Z - 1):
            @pl.when(jnp.logical_and(p < Z - 1, t <= p))
            def _():
                t_copy(p, j, 0, t).wait_send()

            @pl.when(jnp.logical_and(p > 0, t <= Z - 1 - p))
            def _():
                t_copy(p, j, 1, t).wait_send()
        for c in range(Z):
            pl.when(c > p)(lambda: s_copy(c, j, 0).wait_send())
            pl.when(c < p)(lambda: s_copy(c, j, 1).wait_send())
        y_copy(j).wait_send()
        y_copy(j).wait_recv()
        return carry

    lax.fori_loop(0, pieces, sent, 0)


def body(arriving, gain, input_weight, output_weight, block_pattern, S, F, Z):
    tokens = arriving[0, 0]
    rows, depth = tokens.shape
    slab, HG, triple, head = input_weight.shape[1:]
    columns = HG * triple * head
    width = output_weight.shape[-1]
    length = rows * Z
    pieces = rows // PIECE
    X = F // 2
    bf16 = jnp.bfloat16
    dma = pltpu.SemaphoreType.DMA
    vmem = pl.BlockSpec(memory_space=pltpu.VMEM)
    anywhere = pl.BlockSpec(memory_space=pl.ANY)
    passed = pl.pallas_call(
        functools.partial(kernel, S, F, Z, HG),
        out_shape=jax.ShapeDtypeStruct((rows, depth), bf16),
        in_specs=[vmem, vmem, anywhere, anywhere, pl.BlockSpec(memory_space=pltpu.SMEM)],
        out_specs=anywhere,
        scratch_shapes=[
            pltpu.VMEM((length, depth), bf16),
            pltpu.VMEM((depth, columns), bf16),
            pltpu.VMEM((F, HG * head, width), bf16),
            pltpu.VMEM((length, columns), bf16),
            pltpu.VMEM((length, length), jnp.float32),
            pltpu.VMEM((Z, rows, depth), bf16),
            pltpu.VMEM((Z, rows, depth), bf16),
            pltpu.VMEM((Z, rows, depth), bf16),
            pltpu.VMEM((rows, HG * head), bf16),
            pltpu.VMEM((rows, depth), bf16),
            pltpu.VMEM((PIECE, depth), jnp.float32),
            dma((2,)),
            dma((2, Z - 1, pieces)),
            dma((2, Z - 1, pieces)),
            dma((2 * X - 1, 2)),
            dma((F, 2)),
            dma((2 * X - 1,)),
            dma((F,)),
            dma((2, Z, pieces)),
            dma((2, Z, pieces)),
            dma((pieces,)),
            dma((pieces,)),
        ],
        compiler_params=pltpu.CompilerParams(
            collective_id=0, has_side_effects=True, vmem_limit_bytes=48 * 1024 * 1024
        ),
    )(
        tokens,
        gain,
        input_weight[0].reshape(slab, columns),
        output_weight[0].reshape(HG * head, width),
        block_pattern[0, 0],
    )
    return passed[None, None]


def solution(mesh):
    in_specs = (
        P("segment", "fsdp", "seq", None),
        P("segment", None),
        P("segment", "fsdp", "seq", None, None),
        P("segment", "seq", None, "fsdp"),
        P("segment", "fsdp", None, None),
    )
    out_specs = P("segment", "fsdp", "seq", None)
    sizes = {"S": mesh.shape["segment"], "F": mesh.shape["fsdp"], "Z": mesh.shape["seq"]}
    return jax.shard_map(
        functools.partial(body, **sizes), mesh=mesh, in_specs=in_specs, out_specs=out_specs, check_vma=False
    )
```

time: 277 us -> 145 us (0.52)
  waiting for transfers between devices: 187 us -> 0 us
  Pallas kernels: 0 us -> 138 us
  local copies, waits for them, and re-layouts: 36.4 us -> 6.54 us
  matrix products: 26.6 us -> 0 us
  between operations: 13.2 us -> 0.04 us
  other arithmetic: 10.8 us -> 0 us
    pallas_call x0 -> x1, Pallas kernels: none -> 138 us  [body(): pl.pallas_call(functools.partial(kernel, S, F, Z, HG), out_shape=jax.Shap...]
    all_gather x3 -> x0, waiting for transfers between devices: 107 us -> none  [the longest x1 59.6 us: body(): lax.all_gather(normed, 'seq', axis=0, tiled=True)]
    reduce_scatter x1 -> x0, waiting for transfers between devices: 61.5 us -> none  [body(): lax.psum_scatter(jnp.dot(mixed_rows, whole_out, preferred_element_type=jn...]
    dot_general x3 -> x0, matrix products: 19.5 us -> none  [the longest x1 9.25 us: body(): jnp.dot(lax.all_gather(normed, 'seq', axis=0, tiled=True), whole_panel, p...]
    ppermute x1 -> x0, waiting for transfers between devices: 17.9 us -> none  [passed_along(): return lax.ppermute(value, axis, pairs)]
    gather x2 -> x0, local copies, waits for them, and re-layouts: 15.2 us -> none  [the longest x1 7.62 us: attend(): jnp.take(value_blocks, pattern_rows, axis=0)]
    select_n x3 -> x0, local copies, waits for them, and re-layouts: 9.54 us -> none  [the longest x2 5.98 us: attend(): jnp.take(value_blocks, pattern_rows, axis=0)]
    sub x1 -> x0, matrix products: 7.16 us -> none  [attend(): exponent = jnp.exp(scores - row_max)]
  transfers between devices with their start and end apart: 5 -> 0, of which waited for: 4 -> 0; matrix products, arithmetic and copies ran while one was open for 23% -> 0% of each run, Pallas kernels for 0% -> 0%
where the time goes in v1:
time: 145 us; the launch traced here: 144 us
  Pallas kernels  138 us (95%)
  local copies, waits for them, and re-layouts  6.54 us (5%)
    pallas_call x1, Pallas kernels, body(): pl.pallas_call(functools.partial(kernel, S, F, Z, HG), out_shape=jax.Shap...  138 us
    unnamed x11, local copies, waits for them, and re-layouts  4.72 us

profile of v1, /device:TPU:18, one launch (start us, length us, event | category | flops | bytes accessed | tf_op | source)
XLA Modules:
  0.0 144.4 jit_solution(11176983045288535750)
XLA Ops:
  0.0 3.7 %copy.8 = bf16[1,512,4,3,128]{1,4,3,2,0:T(8,128)(2,1)} copy(bf16[1,512,4,3,128]{4,2,3,1,0:T(4,128)(2,1)} %param.7) | data formatting | bytes 3145728 | tf_op args[2]
  3.7 0.0 copy-start.3
  3.7 0.0 copy-start
  3.7 0.0 copy-start.1
  3.7 0.0 copy-start.2
  3.8 1.8 %copy.10.w_ref = bf16[512,1536]{1,0:T(8,128)(2,1)S(1)} copy(bf16[512,1536]{0,1:T(8,128)(2,1)} %bitcast.9) | data formatting | bytes 3145728 | tf_op jit(solution)/shard_map/reshape;squeeze | solution.py:355
  5.6 0.0 copy-done.3
  5.6 0.1 copy.9
  5.7 0.0 copy-done
  5.7 0.0 copy-done.1
  5.7 0.0 copy-done.2
  5.7 137.9 %shard_map.55 = bf16[192,2048]{1,0:T(8,128)(2,1)S(1)} custom-call(bf16[192,2048]{1,0:T(8,128)(2,1)S(1)} %bitcast.6, f32[1,2048]{1,0:T(1,128)S(1)} %copy-done.2, bf16[512,1536]{1,0:T(8,128)(2,1)S(1)} %copy.10.w_ref, bf16[512,512]{1,0:T(8,128)(2,1)S(1)} %bitcast.7, s32[24,6]{1,0:T(8,128)S(1)} %bitcast.8), custom_call_target="tpu_custom_call" | custom-call | tf_op jit(solution)/shard_map/pallas_call | solution.py:320
  143.6 0.9 copy.12
Async XLA Ops:
  3.7 1.8 %copy-start.3 = (s32[1,1,24,6]{2,1,3,0:T(1,128)S(1)}, s32[1,1,24,6]{2,1,3,0:T(1,128)}, u32[]{:S(2)}) copy-start(s32[1,1,24,6]{2,1,3,0:T(1,128)} %param.9) | copy-start | bytes 1732
  3.7 1.9 %copy-start = (bf16[1,1,192,2048]{3,2,1,0:T(8,128)(2,1)S(1)}, bf16[1,1,192,2048]{3,2,1,0:T(8,128)(2,1)}, u32[]{:S(2)}) copy-start(bf16[1,1,192,2048]{3,2,1,0:T(8,128)(2,1)} %param.5) | copy-start | bytes 2359300
  3.7 1.9 %copy-start.1 = (bf16[1,4,128,512]{3,2,1,0:T(8,128)(2,1)S(1)}, bf16[1,4,128,512]{3,2,1,0:T(8,128)(2,1)}, u32[]{:S(2)}) copy-start(bf16[1,4,128,512]{3,2,1,0:T(8,128)(2,1)} %param.8) | copy-start | bytes 1572868
  3.7 1.9 %copy-start.2 = (f32[1,2048]{1,0:T(1,128)S(1)}, f32[1,2048]{1,0:T(1,128)}, u32[]{:S(2)}) copy-start(f32[1,2048]{1,0:T(1,128)} %gain_ref.1) | copy-start | bytes 24580

commit v2 on v1

--- a/solution.py
+++ b/solution.py
@@ -223,42 +223,48 @@
         at = pl.ds(pl.multiple_of(j * PIECE, PIECE), PIECE)
         outb[c, at, :] = (outb[c, at, :].astype(f32) + inbox[c, at, :].astype(f32)).astype(jnp.bfloat16)
 
-    def reduce_step(u, carry):
+    def send_all(c, direction):
+        def one(j, inner):
+            s_copy(c, j, direction).start()
+            return inner
+
+        lax.fori_loop(0, pieces, one, 0)
+
+    def share(e, carry):
+        u = lax.div(e, 2)
+        side = lax.rem(e, 2)
         own = u == Z - 1
         right = Z - 1 - u
-        goes_right = jnp.logical_and(jnp.logical_not(own), right > p)
-        goes_left = jnp.logical_and(jnp.logical_not(own), u < p)
-
-        def side_of(side, inner):
-            c = jnp.where(side == 0, jnp.where(own, p, right), u)
-            valid = jnp.where(side == 0, jnp.logical_or(own, goes_right), goes_left)
-            pl.when(valid)(lambda: partial(c))
-            return inner
-
-        lax.fori_loop(0, 2, side_of, 0)
-
-        def one(j, inner):
-            @pl.when(goes_right)
-            def _():
-                @pl.when(p > 0)
-                def _():
-                    s_copy(right, j, 0).wait_recv()
-                    add_in(right, j, in_l)
-                s_copy(right, j, 0).start()
-
-            @pl.when(goes_left)
-            def _():
-                @pl.when(p < Z - 1)
-                def _():
-                    s_copy(u, j, 1).wait_recv()
-                    add_in(u, j, in_r)
-                s_copy(u, j, 1).start()
-            return inner
-
-        lax.fori_loop(0, pieces, one, 0)
-        return carry
-
-    lax.fori_loop(0, Z, reduce_step, 0)
+        c = jnp.where(side == 0, jnp.where(own, p, right), u)
+        valid = jnp.where(side == 0, jnp.logical_or(own, right > p), jnp.logical_and(jnp.logical_not(own), u < p))
+        pl.when(valid)(lambda: partial(c))
+        leaves = jnp.logical_and(valid, jnp.logical_not(own))
+        pl.when(jnp.logical_and(leaves, jnp.logical_and(side == 0, p == 0)))(lambda: send_all(c, 0))
+        pl.when(jnp.logical_and(leaves, jnp.logical_and(side == 1, p == Z - 1)))(lambda: send_all(c, 1))
+        return carry
+
+    lax.fori_loop(0, 2 * Z, share, 0)
+
+    def relay(step, carry):
+        r = step - p
+        l = step - (Z - 1 - p)
+
+        @pl.when(jnp.logical_and(p > 0, jnp.logical_and(r >= 0, r < (Z - 1 - p) * pieces)))
+        def _():
+            c, j = Z - 1 - lax.div(r, pieces), lax.rem(r, pieces)
+            s_copy(c, j, 0).wait_recv()
+            add_in(c, j, in_l)
+            s_copy(c, j, 0).start()
+
+        @pl.when(jnp.logical_and(p < Z - 1, jnp.logical_and(l >= 0, l < p * pieces)))
+        def _():
+            c, j = lax.div(l, pieces), lax.rem(l, pieces)
+            s_copy(c, j, 1).wait_recv()
+            add_in(c, j, in_r)
+            s_copy(c, j, 1).start()
+        return carry
+
+    lax.fori_loop(0, (Z - 1) * pieces + Z, relay, 0)
 
     def finish(j, carry):
         at = pl.ds(pl.multiple_of(j * PIECE, PIECE), PIECE)

time: 145 us -> 126 us (0.87)
  Pallas kernels: 138 us -> 119 us
    pallas_call x1, Pallas kernels: 138 us -> 119 us  [body(): pl.pallas_call(functools.partial(kernel, S, F, Z, HG), out_shape=jax.Shap...]
where the time goes in v2:
time: 126 us
  Pallas kernels  119 us (94%)
  local copies, waits for them, and re-layouts  6.54 us (5%)
    pallas_call x1, Pallas kernels, body(): pl.pallas_call(functools.partial(kernel, S, F, Z, HG), out_shape=jax.Shap...  119 us
    unnamed x11, local copies, waits for them, and re-layouts  4.72 us

profile of v2, /device:TPU:18, one launch (start us, length us, event | category | flops | bytes accessed | tf_op | source)
XLA Modules:
  0.0 125.8 jit_solution(9860778915018333309)
XLA Ops:
  0.0 3.7 %copy.8 = bf16[1,512,4,3,128]{1,4,3,2,0:T(8,128)(2,1)} copy(bf16[1,512,4,3,128]{4,2,3,1,0:T(4,128)(2,1)} %param.7) | data formatting | bytes 3145728 | tf_op args[2]
  3.7 0.0 copy-start.3
  3.7 0.0 copy-start
  3.7 0.0 copy-start.1
  3.7 0.0 copy-start.2
  3.8 1.8 %copy.10.w_ref = bf16[512,1536]{1,0:T(8,128)(2,1)S(1)} copy(bf16[512,1536]{0,1:T(8,128)(2,1)} %bitcast.9) | data formatting | bytes 3145728 | tf_op jit(solution)/shard_map/reshape;squeeze | solution.py:361
  5.6 0.0 copy-done.3
  5.6 0.1 copy.9
  5.7 0.0 copy-done
  5.7 0.0 copy-done.1
  5.7 0.0 copy-done.2
  5.7 119.2 %shard_map.55 = bf16[192,2048]{1,0:T(8,128)(2,1)S(1)} custom-call(bf16[192,2048]{1,0:T(8,128)(2,1)S(1)} %bitcast.6, f32[1,2048]{1,0:T(1,128)S(1)} %copy-done.2, bf16[512,1536]{1,0:T(8,128)(2,1)S(1)} %copy.10.w_ref, bf16[512,512]{1,0:T(8,128)(2,1)S(1)} %bitcast.7, s32[24,6]{1,0:T(8,128)S(1)} %bitcast.8), custom_call_target="tpu_custom_call" | custom-call | tf_op jit(solution)/shard_map/pallas_call | solution.py:326
  124.9 0.9 copy.12
Async XLA Ops:
  3.7 1.8 %copy-start.3 = (s32[1,1,24,6]{2,1,3,0:T(1,128)S(1)}, s32[1,1,24,6]{2,1,3,0:T(1,128)}, u32[]{:S(2)}) copy-start(s32[1,1,24,6]{2,1,3,0:T(1,128)} %param.9) | copy-start | bytes 1732
  3.7 1.9 %copy-start = (bf16[1,1,192,2048]{3,2,1,0:T(8,128)(2,1)S(1)}, bf16[1,1,192,2048]{3,2,1,0:T(8,128)(2,1)}, u32[]{:S(2)}) copy-start(bf16[1,1,192,2048]{3,2,1,0:T(8,128)(2,1)} %param.5) | copy-start | bytes 2359300
  3.7 1.9 %copy-start.1 = (bf16[1,4,128,512]{3,2,1,0:T(8,128)(2,1)S(1)}, bf16[1,4,128,512]{3,2,1,0:T(8,128)(2,1)}, u32[]{:S(2)}) copy-start(bf16[1,4,128,512]{3,2,1,0:T(8,128)(2,1)} %param.8) | copy-start | bytes 1572868
  3.7 1.9 %copy-start.2 = (f32[1,2048]{1,0:T(1,128)S(1)}, f32[1,2048]{1,0:T(1,128)}, u32[]{:S(2)}) copy-start(f32[1,2048]{1,0:T(1,128)} %gain_ref.1) | copy-start | bytes 24580

commit v3 on v2

--- a/solution.py
+++ b/solution.py
@@ -10,6 +10,8 @@
 BLOCK = 32
 SEL = 6
 PIECE = 32
+STRIP = 32
+PARTS = 4
 EPSILON = 1e-05
 MESH = pl.DeviceIdType.MESH
 
@@ -17,16 +19,17 @@
 def kernel(
     S, F, Z, HG,
     x_ref, gain_ref, w_ref, o_ref, pat_ref, out_ref,
-    tok, win, wout, qkv, bias, in_l, in_r, outb, mixed, fin, acc,
+    raw, tok, win, wout, qkv, bias, in_l, in_r, outb, mixed, fin, acc,
     local_sem, zs, zr, ws, wr, vs, vr, rs, rr, ys, yr,
 ):
     rows, depth = x_ref.shape
     length = rows * Z
-    slab, columns = w_ref.shape
-    head = columns // (3 * HG)
+    slab, head = w_ref.shape[0], w_ref.shape[3]
+    columns = 3 * HG * head
     width = o_ref.shape[1]
     pieces = rows // PIECE
-    half = slab // 2
+    part = slab // PARTS
+    half = o_ref.shape[0] // 2
     X = F // 2
     f32 = jnp.float32
 
@@ -39,8 +42,7 @@
     up = lax.rem(s + 1, S)
     down = lax.rem(s + S - 1, S)
 
-    own_w = pltpu.make_async_copy(
-        w_ref, win.at[pl.ds(pl.multiple_of(f * slab, slab), slab), :], local_sem.at[0])
+    own_w = pltpu.make_async_copy(w_ref, raw, local_sem.at[0])
     own_o = pltpu.make_async_copy(o_ref, wout.at[f], local_sem.at[1])
     own_w.start()
     own_o.start()
@@ -62,18 +64,18 @@
     pl.semaphore_wait(barrier, always + jnp.where(p > 0, 1, 0) + jnp.where(p < Z - 1, 1, 0))
 
     def w_rows(g, k):
-        return win.at[pl.ds(pl.multiple_of(g * slab + k * half, half), half), :]
-
-    def w_copy(g, k, device, slot, own):
-        src = w_ref.at[pl.ds(k * half, half), :] if own else w_rows(g, k)
-        return pltpu.make_async_remote_copy(
-            src_ref=src, dst_ref=w_rows(g, k), send_sem=ws.at[slot, k], recv_sem=wr.at[g, k],
+        return win.at[pl.ds(pl.multiple_of(g * slab + k * part, part), part), :]
+
+    def w_copy(g, k, device, slot):
+        return pltpu.make_async_remote_copy(
+            src_ref=w_rows(g, k), dst_ref=w_rows(g, k), send_sem=ws.at[slot, k], recv_sem=wr.at[g, k],
             device_id={"fsdp": device}, device_id_type=MESH)
 
-    def o_copy(g, device, slot, own):
-        src = o_ref if own else wout.at[g]
-        return pltpu.make_async_remote_copy(
-            src_ref=src, dst_ref=wout.at[g], send_sem=vs.at[slot], recv_sem=vr.at[g],
+    def o_copy(g, k, device, slot, own=False):
+        at = pl.ds(k * half, half)
+        return pltpu.make_async_remote_copy(
+            src_ref=o_ref.at[at, :] if own else wout.at[g, at, :], dst_ref=wout.at[g, at, :],
+            send_sem=vs.at[slot, k], recv_sem=vr.at[g, k],
             device_id={"fsdp": device}, device_id_type=MESH)
 
     def peer(d):
@@ -82,10 +84,17 @@
     def source(d):
         return lax.rem(chip + X - d, X) * 2 + core
 
-    for k in range(2):
+    def send_o(k):
         for d in range(1, X):
-            w_copy(f, k, peer(d), d - 1, True).start()
-        w_copy(f, k, sibling, X - 1, True).start()
+            o_copy(f, k, peer(d), d - 1, True).start()
+        o_copy(f, k, sibling, X - 1, True).start()
+
+    def forward_o(k):
+        for d in range(1, X):
+            o_copy(source(d), k, sibling, X - 1 + d).wait_recv()
+            o_copy(source(d), k, sibling, X - 1 + d).start()
+
+    send_o(0)
 
     def t_rows(c, j):
         return tok.at[pl.ds(pl.multiple_of(c * rows + j * PIECE, PIECE), PIECE), :]
@@ -106,6 +115,19 @@
         return carry
 
     lax.fori_loop(0, pieces, norm_piece, 0)
+
+    own_w.wait()
+
+    def flatten(i, carry):
+        flat = raw[pl.ds(i * STRIP, STRIP)].astype(f32).reshape(STRIP, columns)
+        win[pl.ds(pl.multiple_of(f * slab + i * STRIP, STRIP), STRIP), :] = flat.astype(jnp.bfloat16)
+        return carry
+
+    for k in range(PARTS):
+        lax.fori_loop(k * (part // STRIP), (k + 1) * (part // STRIP), flatten, 0)
+        for d in range(1, X):
+            w_copy(f, k, peer(d), d - 1).start()
+        w_copy(f, k, sibling, X - 1).start()
 
     key_block = lax.broadcasted_iota(jnp.int32, (BLOCK, length), 1) // BLOCK
 
@@ -137,23 +159,19 @@
 
     def forward_w(k):
         for d in range(1, X):
-            w_copy(source(d), k, sibling, X - 1 + d, False).wait_recv()
-            w_copy(source(d), k, sibling, X - 1 + d, False).start()
-
+            w_copy(source(d), k, sibling, X - 1 + d).wait_recv()
+            w_copy(source(d), k, sibling, X - 1 + d).start()
+
+    share_of = -(-PARTS // (Z - 2))
     for t in range(Z - 2):
         receive(t, True)
-        if t < 2:
-            forward_w(t)
-    for k in range(min(2, Z - 2), 2):
-        forward_w(k)
-    for d in range(1, X):
-        o_copy(f, peer(d), d - 1, True).start()
-    o_copy(f, sibling, X - 1, True).start()
-    own_w.wait()
-    for k in range(2):
+        for k in range(t * share_of, min(PARTS, (t + 1) * share_of)):
+            forward_w(k)
+    send_o(1)
+    forward_o(0)
+    for k in range(PARTS):
         for d in range(X):
-            other = lax.rem(chip + d, X) * 2 + 1 - core
-            w_copy(other, k, sibling, 0, False).wait_recv()
+            w_copy(lax.rem(chip + d, X) * 2 + 1 - core, k, sibling, 0).wait_recv()
 
     def project(e, carry):
         d = lax.div(e, 2)
@@ -180,20 +198,18 @@
 
     lax.fori_loop(0, 2 * Z, project, 0)
 
-    for d in range(1, X):
-        o_copy(source(d), sibling, X - 1 + d, False).wait_recv()
-        o_copy(source(d), sibling, X - 1 + d, False).start()
+    forward_o(1)
     own_o.wait()
-    for d in range(X):
-        o_copy(lax.rem(chip + d, X) * 2 + 1 - core, sibling, 0, False).wait_recv()
+    for k in range(2):
+        for d in range(X):
+            o_copy(lax.rem(chip + d, X) * 2 + 1 - core, k, sibling, 0).wait_recv()
 
     def partial(c):
         at = pl.ds(pl.multiple_of(c * rows, rows), rows)
         for h in range(HG):
-            base = h * 3 * head
-            q = qkv[at, base:base + head]
-            k = qkv[:, base + head:base + 2 * head]
-            v = qkv[:, base + 2 * head:base + 3 * head]
+            q = qkv[at, h * head:(h + 1) * head]
+            k = qkv[:, (HG + h) * head:(HG + h + 1) * head]
+            v = qkv[:, (2 * HG + h) * head:(2 * HG + h + 1) * head]
             scores = lax.dot_general(q, k, (((1,), (1,)), ((), ())), preferred_element_type=f32)
             scores = scores * head ** (-0.5) + bias[at, :]
             exponent = jnp.exp(scores - jnp.max(scores, axis=-1, keepdims=True))
@@ -285,11 +301,11 @@
 
     lax.fori_loop(0, pieces, finish, 0)
 
-    for k in range(2):
-        for slot in range(2 * X - 1):
-            w_copy(f, k, sibling, slot, False).wait_send()
     for slot in range(2 * X - 1):
-        o_copy(f, sibling, slot, False).wait_send()
+        for k in range(PARTS):
+            w_copy(f, k, sibling, slot).wait_send()
+        for k in range(2):
+            o_copy(f, k, sibling, slot).wait_send()
 
     def sent(j, carry):
         for t in range(Z - 1):
@@ -326,9 +342,10 @@
     passed = pl.pallas_call(
         functools.partial(kernel, S, F, Z, HG),
         out_shape=jax.ShapeDtypeStruct((rows, depth), bf16),
-        in_specs=[vmem, vmem, anywhere, anywhere, pl.BlockSpec(memory_space=pltpu.SMEM)],
+        in_specs=[vmem, vmem, pl.BlockSpec(memory_space=pltpu.HBM), pl.BlockSpec(memory_space=pltpu.HBM), pl.BlockSpec(memory_space=pltpu.SMEM)],
         out_specs=anywhere,
         scratch_shapes=[
+            pltpu.VMEM((slab, triple, HG, head), bf16),
             pltpu.VMEM((length, depth), bf16),
             pltpu.VMEM((depth, columns), bf16),
             pltpu.VMEM((F, HG * head, width), bf16),
@@ -343,10 +360,10 @@
             dma((2,)),
             dma((2, Z - 1, pieces)),
             dma((2, Z - 1, pieces)),
+            dma((2 * X - 1, PARTS)),
+            dma((F, PARTS)),
             dma((2 * X - 1, 2)),
             dma((F, 2)),
-            dma((2 * X - 1,)),
-            dma((F,)),
             dma((2, Z, pieces)),
             dma((2, Z, pieces)),
             dma((pieces,)),
@@ -358,7 +375,7 @@
     )(
         tokens,
         gain,
-        input_weight[0].reshape(slab, columns),
+        jnp.swapaxes(input_weight[0], 1, 2),
         output_weight[0].reshape(HG * head, width),
         block_pattern[0, 0],
     )

time: 126 us -> 126 us (level)
    another operation x1 -> x0, local copies, waits for them, and re-layouts: 1.82 us -> none  [body(): input_weight[0].reshape(slab, columns)]
    unnamed x11 -> x10, local copies, waits for them, and re-layouts: 4.72 us -> 5.92 us
where the time goes in v3:
time: 126 us; the launch traced here: 125 us
  Pallas kernels  119 us (94%)
  local copies, waits for them, and re-layouts  5.92 us (5%)
    pallas_call x1, Pallas kernels, body(): pl.pallas_call(functools.partial(kernel, S, F, Z, HG), out_shape=jax.Shap...  119 us
    unnamed x10, local copies, waits for them, and re-layouts  5.92 us

profile of v3, /device:TPU:18, one launch (start us, length us, event | category | flops | bytes accessed | tf_op | source)
XLA Modules:
  0.0 125.1 jit_solution(1074196727338770223)
XLA Ops:
  0.0 0.8 copy.6
  0.8 0.0 copy-start
  0.8 1.4 %copy-done = bf16[1,512,4,3,128]{4,2,3,1,0:T(4,128)(2,1)S(1)} copy-done((bf16[1,512,4,3,128]{4,2,3,1,0:T(4,128)(2,1)S(1)}, bf16[1,512,4,3,128]{4,2,3,1,0:T(4,128)(2,1)}, u32[]{:S(2)}) %copy-start) | copy-done | bytes 1572888
  2.2 0.0 copy-start.1
  2.2 1.1 copy-done.1
  3.3 0.0 copy-start.2
  3.3 1.0 copy-done.2
  4.3 0.0 copy-start.3
  4.3 0.7 copy-done.3
  5.0 119.1 %shard_map.55 = bf16[192,2048]{1,0:T(8,128)(2,1)S(1)} custom-call(bf16[192,2048]{1,0:T(8,128)(2,1)S(1)} %bitcast.9, f32[1,2048]{1,0:T(1,128)S(1)} %copy-done.3, bf16[512,3,4,128]{3,2,1,0:T(4,128)(2,1)S(1)} %bitcast.8, bf16[512,512]{1,0:T(8,128)(2,1)S(1)} %bitcast.10, s32[24,6]{1,0:T(8,128)S(1)} %bitcast.11), custom_call_target="tpu_custom_call" | custom-call | tf_op jit(solution)/shard_map/pallas_call | solution.py:342
  124.2 0.9 copy.8
Async XLA Ops:
  0.8 1.4 %copy-start = (bf16[1,512,4,3,128]{4,2,3,1,0:T(4,128)(2,1)S(1)}, bf16[1,512,4,3,128]{4,2,3,1,0:T(4,128)(2,1)}, u32[]{:S(2)}) copy-start(bf16[1,512,4,3,128]{4,2,3,1,0:T(4,128)(2,1)} %param.7) | copy-start | bytes 4718596
  2.2 1.1 copy-start.1
  3.3 1.0 copy-start.2
  4.3 0.7 copy-start.3

commit v4 on v3

--- a/solution.py
+++ b/solution.py
@@ -18,8 +18,8 @@
 
 def kernel(
     S, F, Z, HG,
-    x_ref, gain_ref, w_ref, o_ref, pat_ref, out_ref,
-    raw, tok, win, wout, qkv, bias, in_l, in_r, outb, mixed, fin, acc,
+    x_hbm, gain_hbm, w_ref, o_ref, pat_ref, out_ref,
+    x_ref, gain_ref, raw, tok, win, wout, qkv, bias, in_l, in_r, outb, mixed, fin, acc,
     local_sem, zs, zr, ws, wr, vs, vr, rs, rr, ys, yr,
 ):
     rows, depth = x_ref.shape
@@ -44,6 +44,10 @@
 
     own_w = pltpu.make_async_copy(w_ref, raw, local_sem.at[0])
     own_o = pltpu.make_async_copy(o_ref, wout.at[f], local_sem.at[1])
+    own_x = pltpu.make_async_copy(x_hbm, x_ref, local_sem.at[2])
+    own_gain = pltpu.make_async_copy(gain_hbm, gain_ref, local_sem.at[3])
+    own_x.start()
+    own_gain.start()
     own_w.start()
     own_o.start()
 
@@ -106,6 +110,9 @@
             send_sem=zs.at[direction, step, j], recv_sem=zr.at[direction, step, j],
             device_id={"seq": device}, device_id_type=MESH)
 
+    own_x.wait()
+    own_gain.wait()
+
     def norm_piece(j, carry):
         values = x_ref[pl.ds(pl.multiple_of(j * PIECE, PIECE), PIECE), :].astype(f32)
         spread = jnp.mean(values * values, axis=-1, keepdims=True)
@@ -132,9 +139,9 @@
     key_block = lax.broadcasted_iota(jnp.int32, (BLOCK, length), 1) // BLOCK
 
     def bias_rows(b, carry):
-        hit = key_block == pat_ref[b, 0]
+        hit = key_block == pat_ref[0, 0, b]
         for i in range(1, SEL):
-            hit = jnp.logical_or(hit, key_block == pat_ref[b, i])
+            hit = jnp.logical_or(hit, key_block == pat_ref[i, 0, b])
         bias[pl.ds(pl.multiple_of(b * BLOCK, BLOCK), BLOCK), :] = jnp.where(hit, 0.0, -1e30)
         return carry
 
@@ -337,14 +344,15 @@
     X = F // 2
     bf16 = jnp.bfloat16
     dma = pltpu.SemaphoreType.DMA
-    vmem = pl.BlockSpec(memory_space=pltpu.VMEM)
     anywhere = pl.BlockSpec(memory_space=pl.ANY)
     passed = pl.pallas_call(
         functools.partial(kernel, S, F, Z, HG),
         out_shape=jax.ShapeDtypeStruct((rows, depth), bf16),
-        in_specs=[vmem, vmem, pl.BlockSpec(memory_space=pltpu.HBM), pl.BlockSpec(memory_space=pltpu.HBM), pl.BlockSpec(memory_space=pltpu.SMEM)],
+        in_specs=[anywhere, anywhere, anywhere, anywhere, pl.BlockSpec(memory_space=pltpu.SMEM)],
         out_specs=anywhere,
         scratch_shapes=[
+            pltpu.VMEM((rows, depth), bf16),
+            pltpu.VMEM((1, depth), jnp.float32),
             pltpu.VMEM((slab, triple, HG, head), bf16),
             pltpu.VMEM((length, depth), bf16),
             pltpu.VMEM((depth, columns), bf16),
@@ -357,7 +365,7 @@
             pltpu.VMEM((rows, HG * head), bf16),
             pltpu.VMEM((rows, depth), bf16),
             pltpu.VMEM((PIECE, depth), jnp.float32),
-            dma((2,)),
+            dma((4,)),
             dma((2, Z - 1, pieces)),
             dma((2, Z - 1, pieces)),
             dma((2 * X - 1, PARTS)),
@@ -370,14 +378,14 @@
             dma((pieces,)),
         ],
         compiler_params=pltpu.CompilerParams(
-            collective_id=0, has_side_effects=True, vmem_limit_bytes=48 * 1024 * 1024
+            collective_id=0, has_side_effects=True, vmem_limit_bytes=63 * 1024 * 1024
         ),
     )(
         tokens,
         gain,
         jnp.swapaxes(input_weight[0], 1, 2),
         output_weight[0].reshape(HG * head, width),
-        block_pattern[0, 0],
+        jnp.transpose(block_pattern[0], (2, 0, 1)),
     )
     return passed[None, None]
 

time: 126 us -> 122 us (0.968)
  local copies, waits for them, and re-layouts: 5.92 us -> 2.09 us
    unnamed x10 -> x1, local copies, waits for them, and re-layouts: 5.92 us -> 2.09 us
where the time goes in v4:
time: 122 us; the launch traced here: 121 us
  Pallas kernels  119 us (98%)
  local copies, waits for them, and re-layouts  2.09 us (2%)
    pallas_call x1, Pallas kernels, body(): pl.pallas_call(functools.partial(kernel, S, F, Z, HG), out_shape=jax.Shap...  119 us

profile of v4, /device:TPU:18, one launch (start us, length us, event | category | flops | bytes accessed | tf_op | source)
XLA Modules:
  0.0 121.1 jit_solution(3165644706379466672)
XLA Ops:
  0.0 119.0 %shard_map.55 = bf16[192,2048]{1,0:T(8,128)(2,1)} custom-call(bf16[192,2048]{1,0:T(8,128)(2,1)} %bitcast.11, f32[1,2048]{1,0:T(1,128)} %gain_hbm.1, bf16[512,3,4,128]{3,2,1,0:T(4,128)(2,1)} %bitcast.10, bf16[512,512]{1,0:T(8,128)(2,1)} %bitcast.12, s32[6,1,24]{2,1,0:T(1,128)} %bitcast.13), custom_call_target="tpu_custom_call" | custom-call | tf_op jit(solution)/shard_map/pallas_call | solution.py:348
  119.0 2.1 %copy.7 = bf16[1,1,192,2048]{3,2,1,0:T(8,128)(2,1)} copy(bf16[1,1,192,2048]{3,2,1,0:T(8,128)(2,1)} %bitcast.9) | data formatting | bytes 1572864

commit v5 on v4

--- a/solution.py
+++ b/solution.py
@@ -9,7 +9,8 @@
 
 BLOCK = 32
 SEL = 6
-PIECE = 32
+PIECE = 64
+SUM = 32
 STRIP = 32
 PARTS = 4
 EPSILON = 1e-05
@@ -28,6 +29,7 @@
     columns = 3 * HG * head
     width = o_ref.shape[1]
     pieces = rows // PIECE
+    sums = rows // SUM
     part = slab // PARTS
     half = o_ref.shape[0] // 2
     X = F // 2
@@ -230,20 +232,20 @@
     def s_copy(c, j, direction):
         device = p + 1 if direction == 0 else p - 1
         inbox = in_l if direction == 0 else in_r
-        at = pl.ds(pl.multiple_of(j * PIECE, PIECE), PIECE)
+        at = pl.ds(pl.multiple_of(j * SUM, SUM), SUM)
         return pltpu.make_async_remote_copy(
             src_ref=outb.at[c, at, :], dst_ref=inbox.at[c, at, :],
             send_sem=rs.at[direction, c, j], recv_sem=rr.at[direction, c, j],
             device_id={"seq": device}, device_id_type=MESH)
 
     def y_copy(j):
-        at = pl.ds(pl.multiple_of(j * PIECE, PIECE), PIECE)
+        at = pl.ds(pl.multiple_of(j * SUM, SUM), SUM)
         return pltpu.make_async_remote_copy(
             src_ref=fin.at[at, :], dst_ref=out_ref.at[at, :], send_sem=ys.at[j], recv_sem=yr.at[j],
             device_id={"segment": up}, device_id_type=MESH)
 
     def add_in(c, j, inbox):
-        at = pl.ds(pl.multiple_of(j * PIECE, PIECE), PIECE)
+        at = pl.ds(pl.multiple_of(j * SUM, SUM), SUM)
         outb[c, at, :] = (outb[c, at, :].astype(f32) + inbox[c, at, :].astype(f32)).astype(jnp.bfloat16)
 
     def send_all(c, direction):
@@ -251,7 +253,7 @@
             s_copy(c, j, direction).start()
             return inner
 
-        lax.fori_loop(0, pieces, one, 0)
+        lax.fori_loop(0, sums, one, 0)
 
     def share(e, carry):
         u = lax.div(e, 2)
@@ -272,25 +274,25 @@
         r = step - p
         l = step - (Z - 1 - p)
 
-        @pl.when(jnp.logical_and(p > 0, jnp.logical_and(r >= 0, r < (Z - 1 - p) * pieces)))
-        def _():
-            c, j = Z - 1 - lax.div(r, pieces), lax.rem(r, pieces)
+        @pl.when(jnp.logical_and(p > 0, jnp.logical_and(r >= 0, r < (Z - 1 - p) * sums)))
+        def _():
+            c, j = Z - 1 - lax.div(r, sums), lax.rem(r, sums)
             s_copy(c, j, 0).wait_recv()
             add_in(c, j, in_l)
             s_copy(c, j, 0).start()
 
-        @pl.when(jnp.logical_and(p < Z - 1, jnp.logical_and(l >= 0, l < p * pieces)))
-        def _():
-            c, j = lax.div(l, pieces), lax.rem(l, pieces)
+        @pl.when(jnp.logical_and(p < Z - 1, jnp.logical_and(l >= 0, l < p * sums)))
+        def _():
+            c, j = lax.div(l, sums), lax.rem(l, sums)
             s_copy(c, j, 1).wait_recv()
             add_in(c, j, in_r)
             s_copy(c, j, 1).start()
         return carry
 
-    lax.fori_loop(0, (Z - 1) * pieces + Z, relay, 0)
+    lax.fori_loop(0, (Z - 1) * sums + Z, relay, 0)
 
     def finish(j, carry):
-        at = pl.ds(pl.multiple_of(j * PIECE, PIECE), PIECE)
+        at = pl.ds(pl.multiple_of(j * SUM, SUM), SUM)
         acc[...] = outb[p, at, :].astype(f32)
 
         @pl.when(p < Z - 1)
@@ -306,7 +308,7 @@
         y_copy(j).start()
         return carry
 
-    lax.fori_loop(0, pieces, finish, 0)
+    lax.fori_loop(0, sums, finish, 0)
 
     for slot in range(2 * X - 1):
         for k in range(PARTS):
@@ -323,6 +325,11 @@
             @pl.when(jnp.logical_and(p > 0, t <= Z - 1 - p))
             def _():
                 t_copy(p, j, 1, t).wait_send()
+        return carry
+
+    lax.fori_loop(0, pieces, sent, 0)
+
+    def sums_sent(j, carry):
         for c in range(Z):
             pl.when(c > p)(lambda: s_copy(c, j, 0).wait_send())
             pl.when(c < p)(lambda: s_copy(c, j, 1).wait_send())
@@ -330,7 +337,7 @@
         y_copy(j).wait_recv()
         return carry
 
-    lax.fori_loop(0, pieces, sent, 0)
+    lax.fori_loop(0, sums, sums_sent, 0)
 
 
 def body(arriving, gain, input_weight, output_weight, block_pattern, S, F, Z):
@@ -341,6 +348,7 @@
     width = output_weight.shape[-1]
     length = rows * Z
     pieces = rows // PIECE
+    sums = rows // SUM
     X = F // 2
     bf16 = jnp.bfloat16
     dma = pltpu.SemaphoreType.DMA
@@ -364,7 +372,7 @@
             pltpu.VMEM((Z, rows, depth), bf16),
             pltpu.VMEM((rows, HG * head), bf16),
             pltpu.VMEM((rows, depth), bf16),
-            pltpu.VMEM((PIECE, depth), jnp.float32),
+            pltpu.VMEM((SUM, depth), jnp.float32),
             dma((4,)),
             dma((2, Z - 1, pieces)),
             dma((2, Z - 1, pieces)),
@@ -372,10 +380,10 @@
             dma((F, PARTS)),
             dma((2 * X - 1, 2)),
             dma((F, 2)),
-            dma((2, Z, pieces)),
-            dma((2, Z, pieces)),
-            dma((pieces,)),
-            dma((pieces,)),
+            dma((2, Z, sums)),
+            dma((2, Z, sums)),
+            dma((sums,)),
+            dma((sums,)),
         ],
         compiler_params=pltpu.CompilerParams(
             collective_id=0, has_side_effects=True, vmem_limit_bytes=63 * 1024 * 1024

time: 122 us -> 121 us (level)
  no operation moved by 1% of the time
where the time goes in v5:
time: 121 us
  Pallas kernels  119 us (98%)
  local copies, waits for them, and re-layouts  2.09 us (2%)
    pallas_call x1, Pallas kernels, body(): pl.pallas_call(functools.partial(kernel, S, F, Z, HG), out_shape=jax.Shap...  119 us

profile of v5, /device:TPU:18, one launch (start us, length us, event | category | flops | bytes accessed | tf_op | source)
XLA Modules:
  0.0 120.8 jit_solution(6022454098957919270)
XLA Ops:
  0.0 118.7 %shard_map.55 = bf16[192,2048]{1,0:T(8,128)(2,1)} custom-call(bf16[192,2048]{1,0:T(8,128)(2,1)} %bitcast.11, f32[1,2048]{1,0:T(1,128)} %gain_hbm.1, bf16[512,3,4,128]{3,2,1,0:T(4,128)(2,1)} %bitcast.10, bf16[512,512]{1,0:T(8,128)(2,1)} %bitcast.12, s32[6,1,24]{2,1,0:T(1,128)} %bitcast.13), custom_call_target="tpu_custom_call" | custom-call | tf_op jit(solution)/shard_map/pallas_call | solution.py:356
  118.7 2.1 %copy.7 = bf16[1,1,192,2048]{3,2,1,0:T(8,128)(2,1)} copy(bf16[1,1,192,2048]{3,2,1,0:T(8,128)(2,1)} %bitcast.9) | data formatting | bytes 1572864
